TPU v7x, 1024 devices: a whole 4x4x32 slice. The times are simulated.
1024 devices in a mesh: op: 128 (over x, z), bond: 8 (over y, core).
Axes of the slice: x: 4, y: 4, z: 32, core: 2. Of those that a mesh axis runs over, the one named last changes fastest.
Arguments:
- left_env: bfloat16 [384, 32, 256, 256], P('op', 'bond'), may hold values from -6 to 6
- site_tensor: bfloat16 [32, 1024, 256], P('bond', 'op'), may hold values from -0.375 to 0.375
- sec_sizes: int32 [32], replicated, may hold values from 64 to 256, as said below
- coupling_values: float32 [384, 6], P('op'), may hold values from -4 to 4
- coupling_mask: int32 [384, 6], P('op'), may hold values 0 or 1
Outputs:
- new_env: bfloat16 [384, 32, 256, 256], P('op', 'bond')
Inputs may be any that keep to these rules, and one draw needn't show every extreme that they name: `sec_sizes`: one sector has exactly 256 live rows in every draw.
All inputs are finite; a program needn't handle non-finite values. No bound on the sum of `coupling_mask` on one device may be relied on, other than what follows from the above.
Results may differ from a plain program's by a relative error of at most 0.0057.
Values may be sent and summed in bfloat16 or wider, within the bound.
A program may use at most 64 MiB of HBM per device.

v0:
```python
import jax
import jax.numpy as jnp
from jax import lax
from jax.sharding import PartitionSpec as P

PHYS = 4


CHANNELS = ((0, 1), (1, 3), (3, 4))


def from_behind(x, axis, by):
    size = lax.axis_size(axis)
    pairs = [(i, i + by) for i in range(size) if 0 <= i + by < size]
    return lax.ppermute(x, axis, pairs)


def keep_mask(lengths, block_size):
    positions = jnp.arange(block_size, dtype=jnp.int32)
    return positions[None, :] < lengths[:, None]


def channel_term(environment, chosen, mixing):
    states = chosen.shape[1]
    mixed = []
    for p in range(states):
        summed = mixing[:, p, 0][:, None, None, None] * chosen[None, :, 0]
        for q in range(1, states):
            summed = summed + mixing[:, p, q][:, None, None, None] * chosen[None, :, q]
        mixed.append(summed)
    mixed = jnp.stack(mixed, 2).astype(jnp.bfloat16)
    product = jnp.einsum(
        "omab,ompbc->ompac", environment, mixed, preferred_element_type=jnp.float32
    ).astype(jnp.bfloat16)
    return jnp.einsum("mpab,ompac->ombc", chosen, product, preferred_element_type=jnp.float32)


def local(left_env, site_tensor, sec_sizes, coupling_values, coupling_mask):
    op_count = left_env.shape[0]
    sec_count = left_env.shape[1]
    block_size = left_env.shape[3]
    lowest = lax.axis_index("bond") * sec_count
    padded = jnp.concatenate([jnp.zeros((2,), jnp.int32), sec_sizes, jnp.zeros((2,), jnp.int32)])
    window = lax.dynamic_slice_in_dim(padded, lowest, sec_count + 4)
    coeffs = coupling_values * coupling_mask.astype(jnp.float32)
    mixings = (
        coeffs[:, 0:1].reshape(op_count, 1, 1),
        coeffs[:, 1:5].reshape(op_count, 2, 2),
        coeffs[:, 5:6].reshape(op_count, 1, 1),
    )
    offset = 2
    site_full = lax.all_gather(site_tensor, "op", axis=1, tiled=True)
    extent = site_full.shape[0]
    blocks = site_full.reshape(extent, PHYS, block_size, block_size)
    row_keep = keep_mask(window[offset : offset + extent], block_size)
    env_kept = jnp.where(
        row_keep[None, :, :, None] & row_keep[None, :, None, :],
        left_env,
        jnp.zeros((), left_env.dtype),
    )
    channel_terms = []
    for n, (lower_state, upper_state) in enumerate(CHANNELS):
        begin_at = 0
        col_keep = keep_mask(
            window[offset + begin_at + n : offset + begin_at + n + sec_count], block_size
        )
        kept_mask = row_keep[:, None, :, None] & col_keep[:, None, None, :]
        chosen = jnp.where(
            kept_mask,
            blocks[begin_at : begin_at + sec_count, lower_state:upper_state],
            jnp.zeros((), blocks.dtype),
        )
        channel_terms.append(channel_term(env_kept, chosen, mixings[n]))
    outgoing = jnp.stack(
        [channel_terms[1][:, -1] + channel_terms[2][:, -2], channel_terms[2][:, -1]], 1
    )
    incoming = from_behind(outgoing, "bond", 1)
    zero_one = jnp.zeros((op_count, 1, block_size, block_size), jnp.float32)
    zero_two = jnp.zeros((op_count, 2, block_size, block_size), jnp.float32)
    zero_rest = jnp.zeros((op_count, sec_count - 2, block_size, block_size), jnp.float32)
    totals = channel_terms[0]
    totals = totals + jnp.concatenate([zero_one, channel_terms[1][:, :-1]], 1)
    totals = totals + jnp.concatenate([zero_two, channel_terms[2][:, :-2]], 1)
    totals = totals + jnp.concatenate([incoming, zero_rest], 1)
    return totals.astype(jnp.bfloat16)


def solution(mesh):
    placed = (P("op", "bond", None, None), P("bond", "op", None), P(), P("op", None), P("op", None))
    return jax.shard_map(
        local, mesh=mesh, in_specs=placed, out_specs=P("op", "bond", None, None), check_vma=False
    )
```

profile of v0, /device:TPU:1, one launch (start us, length us, event | category | flops | bytes accessed | tf_op | source)
XLA Modules:
  0.0 331.0 jit_solution(2338186746849538316)
XLA Ops:
  6.5 0.7 all-gather.2.cloned.1.call-update
  7.3 0.7 convert_multiply_fusion
  8.0 0.1 slice.66
  8.0 0.1 copy.9
  8.1 0.7 pad_add_fusion
  8.9 0.1 dynamic_slice.3
  8.9 0.2 slice_reduce_fusion.1
  9.1 0.1 fusion.41
  9.2 0.1 iota_compare_fusion.1
  9.3 0.1 iota_compare_fusion
  9.3 0.3 broadcast_and_fusion
  9.7 246.9 %all-gather.2.cloned.1.call-done = bf16[4,1024,256]{2,1,0:T(8,128)(2,1)} async-done(((bf16[4,8,256]{2,1,0:T(8,128)(2,1)}), bf16[4,1024,256]{2,1,0:T(8,128)(2,1)}) %all-gather.2.cloned.1.call-update) | async-done | bytes 2097168 | tf_op jit(solution)/shard_map/all_gather | solution.py:52
  256.5 1.3 slice_select_fusion
  257.9 1.6 fusion.32
  259.5 0.1 copy-done.4
  259.5 1.1 copy-done.5
  260.6 1.3 bitcast_convert_fusion.1
  261.9 0.3 copy.11
  262.2 2.0 fusion.26
  264.3 0.0 copy-start.1
  264.3 1.9 convolution_bitcast_fusion
  266.2 2.7 add_convert_fusion.1
  268.9 6.2 %fusion.12 = f32[3,4,256,256]{2,3,0,1:T(8,128)} fusion(bf16[4,2,256,256]{3,2,1,0:T(8,128)(2,1)} %copy-done.4, bf16[3,4,1,256,256]{4,3,2,1,0:T(8,128)(2,1)} %get-tuple-element.12, bf16[3,4,1,256,256]{4,3,2,1,0:T(8,128)(2,1)} %get-tuple-element.11, bf16[3,4,256,256]{3,2,1,0:T(8,128)(2,1)} %param.5, pred[4,256,256]{2,1,0:T(8,128)(4,1)S(1)} %get-tuple-element.20), kind=kOutput, calls=%fused_computation.14 | convolution fusion | flops 1614544896 | bytes 9175040 | tf_op jit(solution)/shard_map/mpab,ompac->ombc/dot_general | solution.py:35
  275.1 1.3 slice_add_fusion
  276.4 1.2 pad_maximum_fusion.1
  277.7 24.9 %collective-permute-start = (f32[3,2,256,256]{2,3,0,1:T(8,128)}, f32[3,2,256,256]{2,3,0,1:T(8,128)}, u32[]{:S(2)}, u32[]{:S(2)}) collective-permute-start(f32[3,2,256,256]{2,3,0,1:T(8,128)} %pad_maximum_fusion.1), channel_id=1, source_target_pairs={{0,1},{1,2},{2,3},{3,4},{4,5},{5,6},{6,7},{8,9},{9,10},{10,11},{11... | collective-permute-start | bytes 4718600 | tf_op jit(solution)/shard_map/ppermute | solution.py:15
  302.6 1.2 copy-done.3
  303.8 0.3 copy.7
  304.2 2.2 fusion.25
  306.4 13.9 %collective-permute-done = f32[3,2,256,256]{2,3,0,1:T(8,128)} collective-permute-done((f32[3,2,256,256]{2,3,0,1:T(8,128)}, f32[3,2,256,256]{2,3,0,1:T(8,128)}, u32[]{:S(2)}, u32[]{:S(2)}) %collective-permute-start) | collective-permute-done | bytes 1572896 | tf_op jit(solution)/shard_map/ppermute | solution.py:15
  320.3 2.3 fusion.4
  322.5 1.6 copy.13
  (15 shorter events, 0.0 us)
Async XLA Ops:
  6.5 250.0 %all-gather.2.cloned.1.call-start = ((), (), s32[]{:S(2)}) async-start(), calls=%async_computation | async-start | bytes 2113536 | tf_op jit(solution)/shard_map/all_gather | solution.py:52
  257.9 1.7 copy-start.4
  257.9 2.7 copy-start.5
  264.3 1.9 copy-start.1
  264.3 1.9 copy-start.2
  266.2 36.4 %copy-start = (f32[3,4,256,256]{2,3,0,1:T(8,128)}, f32[3,4,256,256]{2,3,0,1:T(8,128)S(1)}, u32[]{:S(2)}) copy-start(f32[3,4,256,256]{2,3,0,1:T(8,128)S(1)} %convolution_bitcast_fusion) | copy-start | bytes 9437188
  277.7 42.6 %collective-permute-start = (f32[3,2,256,256]{2,3,0,1:T(8,128)}, f32[3,2,256,256]{2,3,0,1:T(8,128)}, u32[]{:S(2)}, u32[]{:S(2)}) collective-permute-start(f32[3,2,256,256]{2,3,0,1:T(8,128)} %pad_maximum_fusion.1), channel_id=1, source_target_pairs={{0,1},{1,2},{2,3},{3,4},{4,5},{5,6},{6,7},{8,9},{9,10},{10,11},{11... | collective-permute-start | bytes 4718600 | tf_op jit(solution)/shard_map/ppermute | solution.py:15
  302.6 1.2 copy-start.3
  304.2 16.1 %slice-start = ((f32[3,4,256,256]{2,3,0,1:T(8,128)}), f32[3,2,256,256]{2,3,0,1:T(8,128)S(1)}, s32[]{:S(2)}) async-start(f32[3,4,256,256]{2,3,0,1:T(8,128)} %copy-done), calls=%async_computation.1 | async-start | bytes 3145728 | tf_op jit(solution)/shard_map/slice | solution.py:83
  304.2 16.1 %slice-start.1 = ((f32[3,4,256,256]{2,3,0,1:T(8,128)}), f32[3,3,256,256]{2,3,0,1:T(8,128)S(1)}, s32[]{:S(2)}) async-start(f32[3,4,256,256]{2,3,0,1:T(8,128)} %fusion.12), calls=%async_computation.2 | async-start | bytes 4718592 | tf_op jit(solution)/shard_map/slice | solution.py:82
Sparse Core Ops, SparseCore 0:
  11.4 245.0 all-gather.1
where the time goes:
time: 331 us
  waiting for transfers between devices  261 us (79%)
  starting transfers between devices  24.9 us (8%)
  matrix products  14.5 us (4%)
  between operations  13.6 us (4%)
  other arithmetic  11.4 us (3%)
  local copies, waits for them, and re-layouts  5.1 us (2%)
    all_gather x1, waiting for transfers between devices, local(): site_full = lax.all_gather(site_tensor, 'op', axis=1, tiled=True)  247 us
    ppermute x1, starting transfers between devices, from_behind(): return lax.ppermute(x, axis, pairs)  24.9 us
    ppermute x1, waiting for transfers between devices, from_behind(): return lax.ppermute(x, axis, pairs)  13.9 us
    dot_general x3, matrix products, channel_term(): jnp.einsum('mpab,ompac->ombc', chosen, product, preferred_element_type=jn...  10.3 us
  transfers between devices with their start and end apart: 2, of which 2 were waited for; matrix products, arithmetic and copies ran while one was open for 1% of the time, Pallas kernels for 0%

commit v1 on v0

v1 whole, which is shorter than its diff:
```python
import functools

import jax
import jax.numpy as jnp
from jax import lax
from jax.experimental import pallas as pl
from jax.experimental.pallas import tpu as pltpu
from jax.sharding import PartitionSpec as P

MESH = pl.DeviceIdType.MESH
NX, NZ, NB = 4, 32, 8
SLOTS, OPS, DIM = 4, 3, 256
ROOT = 15

PLAN = (
    (0, 15, (11, 19, 47, 110, 49, 14, 16, 45, 79, 111)),
    (0, 47, (48,)),
    (0, 14, (12, 46)),
    (0, 16, (18, 17, 112)),
    (0, 111, ()),
    (0, 110, (77, 109)),
    (0, 79, ()),
    (0, 49, (50, 81)),
    (0, 11, (7, 75, 10, 43, 107)),
    (0, 19, (27, 119, 20, 115)),
    (0, 45, ()),
    (0, 48, (78,)),
    (0, 46, ()),
    (0, 112, ()),
    (0, 17, ()),
    (0, 12, (44, 108)),
    (0, 18, (114,)),
    (0, 109, ()),
    (0, 77, (13, 76)),
    (0, 50, (82,)),
    (0, 81, (113,)),
    (0, 43, ()),
    (0, 10, (8, 9, 74, 42, 106)),
    (0, 20, (52, 53, 116)),
    (0, 107, ()),
    (0, 115, (117, 51, 83)),
    (0, 75, (73,)),
    (0, 44, ()),
    (0, 108, ()),
    (0, 7, (3, 39, 4, 103)),
    (0, 114, ()),
    (0, 78, (80,)),
    (0, 82, ()),
    (0, 76, ()),
    (0, 113, ()),
    (0, 13, ()),
    (0, 119, (120, 24, 22, 87, 55, 121, 23)),
    (0, 9, (105,)),
    (0, 106, ()),
    (0, 52, (84,)),
    (0, 116, ()),
    (0, 42, ()),
    (0, 8, (104,)),
    (0, 83, ()),
    (0, 73, (41, 72)),
    (0, 117, (21,)),
    (0, 74, ()),
    (0, 27, (30, 123, 28, 26, 61, 91, 59)),
    (0, 103, (101, 71)),
    (0, 39, (38,)),
    (0, 53, ()),
    (0, 51, ()),
    (0, 120, (88,)),
    (0, 87, (86,)),
    (0, 4, (36, 5, 100)),
    (0, 105, ()),
    (0, 80, ()),
    (0, 23, ()),
    (0, 3, (2, 97, 0, 99, 35)),
    (0, 104, ()),
    (0, 24, (56, 25)),
    (0, 84, (85,)),
    (0, 22, (54, 118)),
    (0, 121, ()),
    (0, 55, ()),
    (0, 41, (40,)),
    (0, 72, ()),
    (0, 21, ()),
    (0, 123, (124, 125)),
    (0, 28, (60,)),
    (0, 71, ()),
    (0, 38, (70, 6)),
    (0, 59, ()),
    (0, 26, (58, 122)),
    (0, 88, (89,)),
    (0, 101, (69,)),
    (0, 30, (126, 95, 63, 29, 31, 62)),
    (0, 91, ()),
    (0, 36, (37, 68)),
    (0, 86, ()),
    (0, 100, ()),
    (0, 5, ()),
    (0, 2, (1,)),
    (0, 56, (57,)),
    (0, 61, ()),
    (0, 35, (34, 67)),
    (0, 99, (66, 98)),
    (0, 25, ()),
    (0, 40, ()),
    (0, 54, ()),
    (0, 118, ()),
    (0, 85, ()),
    (0, 60, (92,)),
    (0, 124, (93,)),
    (0, 6, ()),
    (0, 70, (102,)),
    (0, 97, (64, 65, 96)),
    (0, 122, ()),
    (0, 58, ()),
    (0, 89, (90,)),
    (0, 0, (32,)),
    (0, 69, ()),
    (0, 125, ()),
    (0, 29, ()),
    (0, 126, (94, 127)),
    (0, 31, ()),
    (0, 62, ()),
    (0, 1, (33,)),
    (0, 37, ()),
    (0, 68, ()),
    (0, 34, ()),
    (0, 57, ()),
    (0, 98, ()),
    (0, 63, ()),
    (0, 67, ()),
    (0, 95, ()),
    (0, 92, ()),
    (0, 66, ()),
    (0, 102, ()),
    (0, 96, ()),
    (0, 90, ()),
    (0, 32, ()),
    (0, 65, ()),
    (0, 93, ()),
    (0, 64, ()),
    (0, 94, ()),
    (0, 127, ()),
    (0, 33, ()),
)


def offset(node):
    return (node // NZ, node % NZ - ROOT)


def kernel(
    groups, env_ref, site_ref, sizes_ref, values_ref, mask_ref, out_ref,
    bufs, stage, env, nat, tra, mixed,
    recv_sems, send_sems, own_send, own_recv, halo_send, halo_recv, env_sem,
):
    op, bond = lax.axis_index("op"), lax.axis_index("bond")
    x, z = op // NZ, op % NZ
    shift = (x + 1) // 2
    next_bond = lax.rem(bond + 1, NB)
    last_bond = lax.rem(bond + NB - 1, NB)
    lists = {(g, n): c for g, n, c in PLAN}

    def device(dx, dz, b):
        return (lax.rem(x + dx + 2 * NX, NX) * NZ + lax.rem(z + dz + 2 * NZ, NZ), b)

    first = sorted({c for g in range(len(groups)) for c in lists[(g, ROOT)]})
    barrier = pltpu.get_barrier_semaphore()
    pl.semaphore_signal(barrier, inc=1, device_id=(op, last_bond), device_id_type=MESH)
    for child in first:
        dx, dz = offset(child)
        pl.semaphore_signal(barrier, inc=1, device_id=device(-dx, -dz, bond), device_id_type=MESH)
        pl.semaphore_signal(barrier, inc=1, device_id=device(-dx, -dz, last_bond), device_id_type=MESH)

    own_env = pltpu.make_async_copy(env_ref, env.at[:, 2:6], env_sem)
    own_env.start()

    rows = lax.broadcasted_iota(jnp.int32, (8, DIM), 0) + z * 8
    cols = lax.broadcasted_iota(jnp.int32, (8, DIM), 1)
    for k in range(SLOTS):
        at = lax.rem(k - shift + SLOTS, SLOTS)
        left = bond * SLOTS + at
        right = left + shift
        height = sizes_ref[left]
        width = jnp.where(right < NB * SLOTS, sizes_ref[lax.rem(right, NB * SLOTS)], 0)
        block = site_ref[at].astype(jnp.float32)
        block = jnp.where((rows < height) & (cols < width), block, 0.0)
        stage[k] = jnp.concatenate([block[:, :128], block[:, 128:]], axis=0).astype(jnp.bfloat16)

    pl.semaphore_wait(barrier, 2 * len(first) + 1)

    def target_bond(k):
        return jnp.where(k < shift, next_bond, bond)

    def slot_of(k):
        for g, (lo, hi) in enumerate(groups):
            if lo <= k < hi:
                return g, k - lo

    for g, (lo, hi) in enumerate(groups):
        for child in lists[(g, ROOT)]:
            dx, dz = offset(child)
            parts = [(k, k + 1, target_bond(k)) for k in range(lo, min(hi, 2))]
            if hi > 2:
                parts.append((max(lo, 2), hi, bond))
            for a, b, t in parts:
                pltpu.make_async_remote_copy(
                    src_ref=stage.at[pl.ds(a, b - a)],
                    dst_ref=bufs[g].at[child, pl.ds(a - lo, b - a)],
                    send_sem=send_sems.at[g], recv_sem=recv_sems.at[g, child],
                    device_id=device(dx, dz, t), device_id_type=MESH,
                ).start()

    def own_copy(k):
        g, i = slot_of(k)
        return pltpu.make_async_remote_copy(
            src_ref=stage.at[k], dst_ref=bufs[g].at[ROOT, i],
            send_sem=own_send.at[k], recv_sem=own_recv.at[k],
            device_id=(op, next_bond), device_id_type=MESH,
        )

    halo = pltpu.make_async_remote_copy(
        src_ref=env_ref.at[:, 2:4], dst_ref=env.at[:, 0:2],
        send_sem=halo_send, recv_sem=halo_recv,
        device_id=(op, next_bond), device_id_type=MESH,
    )
    for k in range(2):
        @pl.when(k < shift)
        def _():
            own_copy(k).start()
    halo.start()
    for k in range(SLOTS):
        g, i = slot_of(k)
        if k < 2:
            @pl.when(k >= shift)
            def _():
                bufs[g][ROOT, i] = stage[k]
        else:
            bufs[g][ROOT, i] = stage[k]

    def copy(g, node, child):
        (ax, az), (bx, bz) = offset(node), offset(child)
        return pltpu.make_async_remote_copy(
            src_ref=bufs[g].at[node], dst_ref=bufs[g].at[child],
            send_sem=send_sems.at[g], recv_sem=recv_sems.at[g, child],
            device_id=device(bx - ax, bz - az, bond), device_id_type=MESH,
        )

    for g, node, children in PLAN:
        if node == ROOT:
            continue
        copy(g, node, node if not children else node).wait_recv()
        for child in children:
            copy(g, node, child).start()

    own_env.wait()
    for k in range(2):
        @pl.when(k < shift)
        def _():
            own_copy(k).wait_recv()
    halo.wait_recv()

    for k in range(SLOTS):
        g, i = slot_of(k)

        @pl.loop(0, NZ // 2)
        def _(m):
            for s in range(4):
                base = lax.rem(x - s + NX, NX) * NZ
                tiles = []
                for h in range(2):
                    j = lax.rem(z + ROOT - (2 * m + h) + 2 * NZ, NZ)
                    tiles.append(bufs[g][base + j, i].astype(jnp.float32))
                at = pl.ds(pl.multiple_of(m * 16, 16), 16)
                for half in range(2):
                    cut = slice(half * 8, half * 8 + 8)
                    nat[s, at, half * 128:half * 128 + 128] = jnp.concatenate(
                        [tiles[0][cut], tiles[1][cut]], axis=0).astype(jnp.bfloat16)

        for s in range(4):
            tra[:, s * DIM:(s + 1) * DIM] = nat[s].T
        for o in range(OPS):
            c = [values_ref[o, q] * mask_ref[o, q].astype(jnp.float32) for q in range(6)]

            def product(e, s):
                return jnp.dot(env[o, e], nat[s], preferred_element_type=jnp.float32)

            mixed[0:256] = (c[0] * product(k + 2, 0)).astype(jnp.bfloat16)
            one, two = product(k + 1, 1), product(k + 1, 2)
            mixed[256:512] = (c[1] * one + c[2] * two).astype(jnp.bfloat16)
            mixed[512:768] = (c[3] * one + c[4] * two).astype(jnp.bfloat16)
            mixed[768:1024] = (c[5] * product(k, 3)).astype(jnp.bfloat16)
            out_ref[o, k] = jnp.dot(tra[...], mixed[...], preferred_element_type=jnp.float32).astype(jnp.bfloat16)

    for k in range(2):
        @pl.when(k < shift)
        def _():
            own_copy(k).wait_send()
    halo.wait_send()
    for g in range(len(groups)):
        everything = bufs[g].at[pl.ds(0, NX * NZ - 1)]
        pltpu.make_async_remote_copy(
            src_ref=everything, dst_ref=everything, send_sem=send_sems.at[g], recv_sem=recv_sems.at[g, ROOT],
            device_id=(op, next_bond), device_id_type=MESH,
        ).wait_send()


GROUPS = ((0, 4),)


def body(groups, *refs):
    n = len(groups)
    ins, bufs, rest = refs[:6], refs[6:6 + n], refs[6 + n:]
    kernel(groups, *ins, bufs, *rest)


def local(left_env, site_tensor, sec_sizes, coupling_values, coupling_mask):
    return pl.pallas_call(
        functools.partial(body, GROUPS),
        name="gather_and_renormalize",
        out_shape=jax.ShapeDtypeStruct(left_env.shape, jnp.bfloat16),
        in_specs=[
            pl.BlockSpec(memory_space=pl.ANY),
            pl.BlockSpec(memory_space=pltpu.VMEM),
            pl.BlockSpec(memory_space=pltpu.SMEM),
            pl.BlockSpec(memory_space=pltpu.SMEM),
            pl.BlockSpec(memory_space=pltpu.SMEM),
        ],
        out_specs=pl.BlockSpec(memory_space=pltpu.VMEM),
        scratch_shapes=[pltpu.VMEM((NX * NZ, hi - lo, 16, 128), jnp.bfloat16) for lo, hi in GROUPS] + [
            pltpu.VMEM((SLOTS, 16, 128), jnp.bfloat16),
            pltpu.VMEM((OPS, 6, DIM, DIM), jnp.bfloat16),
            pltpu.VMEM((4, DIM, DIM), jnp.bfloat16),
            pltpu.VMEM((DIM, 4 * DIM), jnp.bfloat16),
            pltpu.VMEM((4 * DIM, DIM), jnp.bfloat16),
            pltpu.SemaphoreType.DMA((len(GROUPS), NX * NZ)),
            pltpu.SemaphoreType.DMA((len(GROUPS),)),
            pltpu.SemaphoreType.DMA((2,)),
            pltpu.SemaphoreType.DMA((2,)),
            pltpu.SemaphoreType.DMA,
            pltpu.SemaphoreType.DMA,
            pltpu.SemaphoreType.DMA,
        ],
        compiler_params=pltpu.CompilerParams(
            collective_id=0, has_side_effects=True, vmem_limit_bytes=60 * 1024 * 1024
        ),
        cost_estimate=pl.CostEstimate(flops=3_221_225_472, bytes_accessed=3_145_728, transcendentals=0),
    )(left_env, site_tensor, sec_sizes, coupling_values, coupling_mask)


def solution(mesh):
    placed = (P("op", "bond", None, None), P("bond", "op", None), P(), P("op", None), P("op", None))
    return jax.shard_map(
        local, mesh=mesh, in_specs=placed, out_specs=P("op", "bond", None, None), check_vma=False
    )
```

time: 331 us -> 62.2 us (0.19)
  the two profiles are of different devices: /device:TPU:1 before, /device:TPU:8 now
where the time goes in v1:
time: 62.2 us; the launch traced here: 62 us
  Pallas kernels  59.3 us (95%)
  local copies, waits for them, and re-layouts  2.65 us (4%)
    pallas_call x1, Pallas kernels, local(): pl.pallas_call(functools.partial(body, GROUPS), name='gather_and_renormal...  59.3 us
    unnamed x1, local copies, waits for them, and re-layouts  2.65 us

profile of v1, /device:TPU:8, one launch (start us, length us, event | category | flops | bytes accessed | tf_op | source)
XLA Modules:
  0.0 62.0 jit_solution(11945501236599135388)
XLA Ops:
  0.0 59.3 %gather_and_renormalize.1 = bf16[3,4,256,256]{3,2,1,0:T(8,128)(2,1)} custom-call(bf16[3,4,256,256]{3,2,1,0:T(8,128)(2,1)} %refs_0_.1, bf16[4,8,256]{2,1,0:T(8,128)(2,1)} %refs_1_.1, s32[32]{0:T(128)} %refs_2_.1, f32[3,6]{1,0:T(4,128)} %refs_3_.1, s32[3,6]{1,0:T(4,128)} %refs_4_.1), custom_call_target="tpu_custom_call" | custom-call | flops 3221225472 | bytes 3145728 | tf_op jit(solution)/shard_map/gather_and_renormalize/pallas_call | solution.py:317
  59.3 2.7 %copy.7 = bf16[3,4,256,256]{3,2,1,0:T(8,128)(2,1)} copy(bf16[3,4,256,256]{3,2,1,0:T(8,128)(2,1)} %gather_and_renormalize.1) | data formatting | bytes 3145728

commit v2 on v1

v2 whole, which is shorter than its diff:
```python
import jax
import jax.numpy as jnp
from jax import lax
from jax.experimental import pallas as pl
from jax.experimental.pallas import tpu as pltpu
from jax.sharding import PartitionSpec as P

MESH = pl.DeviceIdType.MESH
NX, NZ, NB = 4, 32, 8
SLOTS, OPS, DIM = 4, 3, 256
ROOT = 15

PLAN = (
    (0, 15, (11, 19, 47, 110, 49, 14, 16, 45, 79, 111)),
    (0, 47, (48,)),
    (0, 14, (12, 46)),
    (0, 16, (18, 17, 112)),
    (0, 111, ()),
    (0, 110, (77, 109)),
    (0, 79, ()),
    (0, 49, (50, 81)),
    (0, 11, (7, 75, 10, 43, 107)),
    (0, 19, (27, 119, 20, 115)),
    (0, 45, ()),
    (0, 48, (78,)),
    (0, 46, ()),
    (0, 112, ()),
    (0, 17, ()),
    (0, 12, (44, 108)),
    (0, 18, (114,)),
    (0, 109, ()),
    (0, 77, (13, 76)),
    (0, 50, (82,)),
    (0, 81, (113,)),
    (0, 43, ()),
    (0, 10, (8, 9, 74, 42, 106)),
    (0, 20, (52, 53, 116)),
    (0, 107, ()),
    (0, 115, (117, 51, 83)),
    (0, 75, (73,)),
    (0, 44, ()),
    (0, 108, ()),
    (0, 7, (3, 39, 4, 103)),
    (0, 114, ()),
    (0, 78, (80,)),
    (0, 82, ()),
    (0, 76, ()),
    (0, 113, ()),
    (0, 13, ()),
    (0, 119, (120, 24, 22, 87, 55, 121, 23)),
    (0, 9, (105,)),
    (0, 106, ()),
    (0, 52, (84,)),
    (0, 116, ()),
    (0, 42, ()),
    (0, 8, (104,)),
    (0, 83, ()),
    (0, 73, (41, 72)),
    (0, 117, (21,)),
    (0, 74, ()),
    (0, 27, (30, 123, 28, 26, 61, 91, 59)),
    (0, 103, (101, 71)),
    (0, 39, (38,)),
    (0, 53, ()),
    (0, 51, ()),
    (0, 120, (88,)),
    (0, 87, (86,)),
    (0, 4, (36, 5, 100)),
    (0, 105, ()),
    (0, 80, ()),
    (0, 23, ()),
    (0, 3, (2, 97, 0, 99, 35)),
    (0, 104, ()),
    (0, 24, (56, 25)),
    (0, 84, (85,)),
    (0, 22, (54, 118)),
    (0, 121, ()),
    (0, 55, ()),
    (0, 41, (40,)),
    (0, 72, ()),
    (0, 21, ()),
    (0, 123, (124, 125)),
    (0, 28, (60,)),
    (0, 71, ()),
    (0, 38, (70, 6)),
    (0, 59, ()),
    (0, 26, (58, 122)),
    (0, 88, (89,)),
    (0, 101, (69,)),
    (0, 30, (126, 95, 63, 29, 31, 62)),
    (0, 91, ()),
    (0, 36, (37, 68)),
    (0, 86, ()),
    (0, 100, ()),
    (0, 5, ()),
    (0, 2, (1,)),
    (0, 56, (57,)),
    (0, 61, ()),
    (0, 35, (34, 67)),
    (0, 99, (66, 98)),
    (0, 25, ()),
    (0, 40, ()),
    (0, 54, ()),
    (0, 118, ()),
    (0, 85, ()),
    (0, 60, (92,)),
    (0, 124, (93,)),
    (0, 6, ()),
    (0, 70, (102,)),
    (0, 97, (64, 65, 96)),
    (0, 122, ()),
    (0, 58, ()),
    (0, 89, (90,)),
    (0, 0, (32,)),
    (0, 69, ()),
    (0, 125, ()),
    (0, 29, ()),
    (0, 126, (94, 127)),
    (0, 31, ()),
    (0, 62, ()),
    (0, 1, (33,)),
    (0, 37, ()),
    (0, 68, ()),
    (0, 34, ()),
    (0, 57, ()),
    (0, 98, ()),
    (0, 63, ()),
    (0, 67, ()),
    (0, 95, ()),
    (0, 92, ()),
    (0, 66, ()),
    (0, 102, ()),
    (0, 96, ()),
    (0, 90, ()),
    (0, 32, ()),
    (0, 65, ()),
    (0, 93, ()),
    (0, 64, ()),
    (0, 94, ()),
    (0, 127, ()),
    (0, 33, ()),
)


def offset(node):
    return (node // NZ, node % NZ - ROOT)


def gather(
    env_ref, site_in, sizes_in, buf, halo_ref,
    stage, site_ref, sizes_ref,
    recv_sems, leaf_sems, send_sem, own_send, own_recv, halo_send, halo_recv, in_sems,
):
    op, bond = lax.axis_index("op"), lax.axis_index("bond")
    x, z = op // NZ, op % NZ
    shift = (x + 1) // 2
    next_bond = lax.rem(bond + 1, NB)
    last_bond = lax.rem(bond + NB - 1, NB)
    lists = {n: c for _, n, c in PLAN}

    def device(dx, dz, b):
        return (lax.rem(x + dx + 2 * NX, NX) * NZ + lax.rem(z + dz + 2 * NZ, NZ), b)

    first = sorted(lists[ROOT])
    barrier = pltpu.get_barrier_semaphore()
    pl.semaphore_signal(barrier, inc=1, device_id=(op, last_bond), device_id_type=MESH)
    for child in first:
        dx, dz = offset(child)
        pl.semaphore_signal(barrier, inc=1, device_id=device(-dx, -dz, bond), device_id_type=MESH)
        pl.semaphore_signal(barrier, inc=1, device_id=device(-dx, -dz, last_bond), device_id_type=MESH)

    site_copy = pltpu.make_async_copy(site_in, site_ref, in_sems.at[0])
    sizes_copy = pltpu.make_async_copy(sizes_in, sizes_ref, in_sems.at[1])
    for c in (site_copy, sizes_copy):
        c.start()
    site_copy.wait()
    sizes_copy.wait()

    rows = lax.broadcasted_iota(jnp.int32, (8, DIM), 0) + z * 8
    cols = lax.broadcasted_iota(jnp.int32, (8, DIM), 1)
    for k in range(SLOTS):
        at = lax.rem(k - shift + SLOTS, SLOTS)
        left = bond * SLOTS + at
        right = left + shift
        height = sizes_ref[left]
        width = jnp.where(right < NB * SLOTS, sizes_ref[lax.rem(right, NB * SLOTS)], 0)
        block = site_ref[at].astype(jnp.float32)
        block = jnp.where((rows < height) & (cols < width), block, 0.0)
        stage[k] = jnp.concatenate([block[:, :128], block[:, 128:]], axis=0).astype(jnp.bfloat16)

    pl.semaphore_wait(barrier, 2 * len(first) + 1)

    def target_bond(k):
        return jnp.where(k < shift, next_bond, bond)

    def arrival(child):
        return recv_sems.at[child] if lists[child] else leaf_sems.at[child // NZ]

    for child in lists[ROOT]:
        dx, dz = offset(child)
        for lo, hi, to in ((0, 1, target_bond(0)), (1, 2, target_bond(1)), (2, SLOTS, bond)):
            pltpu.make_async_remote_copy(
                src_ref=stage.at[pl.ds(lo, hi - lo)],
                dst_ref=buf.at[child, pl.ds(lo, hi - lo)],
                send_sem=send_sem, recv_sem=arrival(child),
                device_id=device(dx, dz, to), device_id_type=MESH,
            ).start()

    def own_copy(k):
        return pltpu.make_async_remote_copy(
            src_ref=stage.at[k], dst_ref=buf.at[ROOT, k],
            send_sem=own_send.at[k], recv_sem=own_recv.at[k],
            device_id=(op, next_bond), device_id_type=MESH,
        )

    halo = pltpu.make_async_remote_copy(
        src_ref=env_ref.at[:, 2:4], dst_ref=halo_ref,
        send_sem=halo_send, recv_sem=halo_recv,
        device_id=(op, next_bond), device_id_type=MESH,
    )
    for k in range(SLOTS):
        if k < 2:
            @pl.when(k < shift)
            def _():
                own_copy(k).start()

            @pl.when(k >= shift)
            def _():
                buf[ROOT, k] = stage[k]
        else:
            buf[ROOT, k] = stage[k]
    halo.start()

    def copy(node, child):
        (ax, az), (bx, bz) = offset(node), offset(child)
        return pltpu.make_async_remote_copy(
            src_ref=buf.at[node], dst_ref=buf.at[child],
            send_sem=send_sem, recv_sem=arrival(child),
            device_id=device(bx - ax, bz - az, bond), device_id_type=MESH,
        )

    for _, node, children in PLAN:
        if node != ROOT and children:
            copy(node, node).wait_recv()
            for child in children:
                copy(node, child).start()

    for k in range(2):
        @pl.when(k < shift)
        def _():
            own_copy(k).wait_recv()

    for ox in range(NX):
        leaves = sum(1 for n, c in lists.items() if n // NZ == ox and not c)
        if leaves:
            some = buf.at[pl.ds(0, leaves)]
            pltpu.make_async_remote_copy(
                src_ref=some, dst_ref=some, send_sem=send_sem, recv_sem=leaf_sems.at[ox],
                device_id=(op, next_bond), device_id_type=MESH,
            ).wait_recv()
    halo.wait_recv()
    for k in range(2):
        @pl.when(k < shift)
        def _():
            own_copy(k).wait_send()
    halo.wait_send()
    everything = buf.at[pl.ds(0, NX * NZ - 1)]
    pltpu.make_async_remote_copy(
        src_ref=everything, dst_ref=everything, send_sem=send_sem, recv_sem=halo_recv,
        device_id=(op, next_bond), device_id_type=MESH,
    ).wait_send()


def products(own, buf, halo, values_ref, mask_ref, out_ref, nat, tra, mixed, result, sems):
    op = lax.axis_index("op")
    x, z = op // NZ, op % NZ
    tile = [lax.rem(z + ROOT - m + NZ, NZ) for m in range(NZ)]
    plane = [lax.rem(x - s + NX, NX) * NZ for s in range(4)]
    for k in range(SLOTS):
        for s in range(4):
            tiles = [buf[plane[s] + j, k].astype(jnp.float32) for j in tile]
            left = jnp.concatenate([t[:8] for t in tiles], axis=0)
            right = jnp.concatenate([t[8:] for t in tiles], axis=0)
            block = jnp.concatenate([left, right], axis=1).astype(jnp.bfloat16)
            nat[k, s] = block
            tra[k, :, s * DIM:(s + 1) * DIM] = block.T

    def env(o, e):
        return own[o, e] if e >= 0 else halo[o, e + 2]

    copies = []
    for k in range(SLOTS):
        for o in range(OPS):
            c = [values_ref[o, q] * mask_ref[o, q].astype(jnp.float32) for q in range(6)]

            def product(e, s):
                return jnp.dot(env(o, e), nat[k, s], preferred_element_type=jnp.float32)

            mixed[o, 0:256] = (c[0] * product(k, 0)).astype(jnp.bfloat16)
            one, two = product(k - 1, 1), product(k - 1, 2)
            mixed[o, 256:512] = (c[1] * one + c[2] * two).astype(jnp.bfloat16)
            mixed[o, 512:768] = (c[3] * one + c[4] * two).astype(jnp.bfloat16)
            mixed[o, 768:1024] = (c[5] * product(k - 2, 3)).astype(jnp.bfloat16)
            result[o, k] = jnp.dot(tra[k], mixed[o], preferred_element_type=jnp.float32).astype(jnp.bfloat16)
            copies.append(pltpu.make_async_copy(result.at[o, k], out_ref.at[o, k], sems.at[o, k]))
            copies[-1].start()
    for copy in copies:
        copy.wait()


VMEM, SMEM, ANY, HBM = (pl.BlockSpec(memory_space=m) for m in (pltpu.VMEM, pltpu.SMEM, pl.ANY, pltpu.HBM))


def local(left_env, site_tensor, sec_sizes, coupling_values, coupling_mask):
    buf, halo = pl.pallas_call(
        gather,
        name="gather",
        out_shape=[
            pltpu.VMEM((NX * NZ, SLOTS, 16, 128), jnp.bfloat16),
            pltpu.VMEM((OPS, 2, DIM, DIM), jnp.bfloat16),
        ],
        in_specs=[HBM] * 3,
        out_specs=[VMEM] * 2,
        scratch_shapes=[
            pltpu.VMEM((SLOTS, 16, 128), jnp.bfloat16),
            pltpu.VMEM((SLOTS, 8, DIM), jnp.bfloat16),
            pltpu.SMEM((NB * SLOTS,), jnp.int32),
            pltpu.SemaphoreType.DMA((NX * NZ,)),
            pltpu.SemaphoreType.DMA((NX,)),
            pltpu.SemaphoreType.DMA,
            pltpu.SemaphoreType.DMA((2,)),
            pltpu.SemaphoreType.DMA((2,)),
            pltpu.SemaphoreType.DMA,
            pltpu.SemaphoreType.DMA,
            pltpu.SemaphoreType.DMA((2,)),
        ],
        compiler_params=pltpu.CompilerParams(
            collective_id=0, has_side_effects=True, vmem_limit_bytes=56 * 1024 * 1024
        ),
        cost_estimate=pl.CostEstimate(flops=0, bytes_accessed=6_000_000, transcendentals=0),
    )(left_env, site_tensor, sec_sizes)
    return pl.pallas_call(
        products,
        name="products",
        out_shape=jax.ShapeDtypeStruct(left_env.shape, jnp.bfloat16),
        in_specs=[VMEM, VMEM, VMEM, SMEM, SMEM],
        out_specs=HBM,
        scratch_shapes=[
            pltpu.VMEM((SLOTS, 4, DIM, DIM), jnp.bfloat16),
            pltpu.VMEM((SLOTS, DIM, 4 * DIM), jnp.bfloat16),
            pltpu.VMEM((OPS, 4 * DIM, DIM), jnp.bfloat16),
            pltpu.VMEM((OPS, SLOTS, DIM, DIM), jnp.bfloat16),
            pltpu.SemaphoreType.DMA((OPS, SLOTS)),
        ],
        compiler_params=pltpu.CompilerParams(vmem_limit_bytes=32 * 1024 * 1024),
        cost_estimate=pl.CostEstimate(flops=3_221_225_472, bytes_accessed=3_145_728, transcendentals=0),
    )(left_env, buf, halo, coupling_values, coupling_mask)


def solution(mesh):
    placed = (P("op", "bond", None, None), P("bond", "op", None), P(), P("op", None), P("op", None))
    return jax.shard_map(
        local, mesh=mesh, in_specs=placed, out_specs=P("op", "bond", None, None), check_vma=False
    )
```

time: 62.2 us -> 56.5 us (0.908)
  Pallas kernels: 59.3 us -> 56.2 us
  local copies, waits for them, and re-layouts: 2.65 us -> 0.01 us
    pallas_call x1 -> x2, Pallas kernels: 59.3 us -> 56.2 us  [the longest x1 51.1 us: local(): pl.pallas_call(gather, name='gather', out_shape=[pltpu.VMEM((NX * NZ, SLO...]
    unnamed x1 -> x6, local copies, waits for them, and re-layouts: 2.65 us -> 0.01 us
where the time goes in v2:
time: 56.5 us; the launch traced here: 56.3 us
  Pallas kernels  56.2 us (99%)
    pallas_call x1, Pallas kernels, local(): pl.pallas_call(gather, name='gather', out_shape=[pltpu.VMEM((NX * NZ, SLO...  51.1 us
    pallas_call x1, Pallas kernels, local(): pl.pallas_call(products, name='products', out_shape=jax.ShapeDtypeStruct(...  5.15 us

profile of v2, /device:TPU:8, one launch (start us, length us, event | category | flops | bytes accessed | tf_op | source)
XLA Modules:
  0.0 56.3 jit_solution(15781725973017015577)
XLA Ops:
  0.0 0.0 copy-start
  0.0 0.0 copy-start.2
  0.0 0.0 copy-start.1
  0.0 51.1 %gather.1 = (bf16[128,4,16,128]{3,2,1,0:T(8,128)(2,1)S(1)}, bf16[3,2,256,256]{3,2,1,0:T(8,128)(2,1)S(1)}) custom-call(bf16[3,4,256,256]{3,2,1,0:T(8,128)(2,1)} %own.1, bf16[4,8,256]{2,1,0:T(8,128)(2,1)} %site_in.1, s32[32]{0:T(128)} %sizes_in.1), custom_call_target="tpu_custom_call" | custom-call | bytes 6000000 | tf_op jit(solution)/shard_map/gather/pallas_call | solution.py:315
  51.1 0.0 copy-done
  51.1 0.0 copy-done.2
  51.1 0.0 copy-done.1
  51.1 5.1 %products.1 = bf16[3,4,256,256]{3,2,1,0:T(8,128)(2,1)} custom-call(bf16[3,4,256,256]{3,2,1,0:T(8,128)(2,1)S(1)} %copy-done, bf16[128,4,16,128]{3,2,1,0:T(8,128)(2,1)S(1)} %get-tuple-element.7.buf, bf16[3,2,256,256]{3,2,1,0:T(8,128)(2,1)S(1)} %get-tuple-element.8.halo, f32[3,6]{1,0:T(4,128)S(1)} %copy-done.1, s32[3,6]{1,0:T(4,128)S(1)} %copy-done.2), custom_call_target="tpu_custom_call" | custom-call | flops 3221225472 | bytes 3145728 | tf_op jit(solution)/shard_map/products/pallas_call | solution.py:342
Async XLA Ops:
  0.0 51.1 %copy-start = (bf16[3,4,256,256]{3,2,1,0:T(8,128)(2,1)S(1)}, bf16[3,4,256,256]{3,2,1,0:T(8,128)(2,1)}, u32[]{:S(2)}) copy-start(bf16[3,4,256,256]{3,2,1,0:T(8,128)(2,1)} %own.1) | copy-start | bytes 4718596
  0.0 51.1 %copy-start.2 = (s32[3,6]{1,0:T(4,128)S(1)}, s32[3,6]{1,0:T(4,128)}, u32[]{:S(2)}) copy-start(s32[3,6]{1,0:T(4,128)} %mask_ref.1) | copy-start | bytes 220
  0.0 51.1 %copy-start.1 = (f32[3,6]{1,0:T(4,128)S(1)}, f32[3,6]{1,0:T(4,128)}, u32[]{:S(2)}) copy-start(f32[3,6]{1,0:T(4,128)} %values_ref.1) | copy-start | bytes 220

commit v3 on v2

--- a/solution.py
+++ b/solution.py
@@ -161,13 +161,13 @@
     def device(dx, dz, b):
         return (lax.rem(x + dx + 2 * NX, NX) * NZ + lax.rem(z + dz + 2 * NZ, NZ), b)
 
-    first = sorted(lists[ROOT])
+    first = sorted(lists[ROOT], key=lambda c: -abs(offset(c)[1]))
     barrier = pltpu.get_barrier_semaphore()
-    pl.semaphore_signal(barrier, inc=1, device_id=(op, last_bond), device_id_type=MESH)
     for child in first:
         dx, dz = offset(child)
-        pl.semaphore_signal(barrier, inc=1, device_id=device(-dx, -dz, bond), device_id_type=MESH)
-        pl.semaphore_signal(barrier, inc=1, device_id=device(-dx, -dz, last_bond), device_id_type=MESH)
+        for b in (last_bond, bond):
+            pl.semaphore_signal(barrier, inc=1, device_id=device(-dx, -dz, b), device_id_type=MESH)
+    pl.semaphore_signal(barrier, inc=1, device_id=(op, last_bond), device_id_type=MESH)
 
     site_copy = pltpu.make_async_copy(site_in, site_ref, in_sems.at[0])
     sizes_copy = pltpu.make_async_copy(sizes_in, sizes_ref, in_sems.at[1])
@@ -190,21 +190,22 @@
 
     pl.semaphore_wait(barrier, 2 * len(first) + 1)
 
-    def target_bond(k):
-        return jnp.where(k < shift, next_bond, bond)
-
     def arrival(child):
         return recv_sems.at[child] if lists[child] else leaf_sems.at[child // NZ]
 
-    for child in lists[ROOT]:
-        dx, dz = offset(child)
-        for lo, hi, to in ((0, 1, target_bond(0)), (1, 2, target_bond(1)), (2, SLOTS, bond)):
-            pltpu.make_async_remote_copy(
-                src_ref=stage.at[pl.ds(lo, hi - lo)],
-                dst_ref=buf.at[child, pl.ds(lo, hi - lo)],
-                send_sem=send_sem, recv_sem=arrival(child),
-                device_id=device(dx, dz, to), device_id_type=MESH,
-            ).start()
+    for moved in range(3):
+        @pl.when(shift == moved)
+        def _():
+            for child in lists[ROOT]:
+                dx, dz = offset(child)
+                for lo, hi, to in ((0, moved, next_bond), (moved, SLOTS, bond)):
+                    if lo < hi:
+                        pltpu.make_async_remote_copy(
+                            src_ref=stage.at[pl.ds(lo, hi - lo)],
+                            dst_ref=buf.at[child, pl.ds(lo, hi - lo)],
+                            send_sem=send_sem, recv_sem=arrival(child),
+                            device_id=device(dx, dz, to), device_id_type=MESH,
+                        ).start()
 
     def own_copy(k):
         return pltpu.make_async_remote_copy(
@@ -288,22 +289,27 @@
     def env(o, e):
         return own[o, e] if e >= 0 else halo[o, e + 2]
 
+    def mix(k, o, at):
+        c = [values_ref[o, q] * mask_ref[o, q].astype(jnp.float32) for q in range(6)]
+
+        def product(e, s):
+            return jnp.dot(env(o, e), nat[k, s], preferred_element_type=jnp.float32)
+
+        mixed[at, 0:256] = (c[0] * product(k, 0)).astype(jnp.bfloat16)
+        one, two = product(k - 1, 1), product(k - 1, 2)
+        mixed[at, 256:512] = (c[1] * one + c[2] * two).astype(jnp.bfloat16)
+        mixed[at, 512:768] = (c[3] * one + c[4] * two).astype(jnp.bfloat16)
+        mixed[at, 768:1024] = (c[5] * product(k - 2, 3)).astype(jnp.bfloat16)
+
     copies = []
-    for k in range(SLOTS):
-        for o in range(OPS):
-            c = [values_ref[o, q] * mask_ref[o, q].astype(jnp.float32) for q in range(6)]
-
-            def product(e, s):
-                return jnp.dot(env(o, e), nat[k, s], preferred_element_type=jnp.float32)
-
-            mixed[o, 0:256] = (c[0] * product(k, 0)).astype(jnp.bfloat16)
-            one, two = product(k - 1, 1), product(k - 1, 2)
-            mixed[o, 256:512] = (c[1] * one + c[2] * two).astype(jnp.bfloat16)
-            mixed[o, 512:768] = (c[3] * one + c[4] * two).astype(jnp.bfloat16)
-            mixed[o, 768:1024] = (c[5] * product(k - 2, 3)).astype(jnp.bfloat16)
-            result[o, k] = jnp.dot(tra[k], mixed[o], preferred_element_type=jnp.float32).astype(jnp.bfloat16)
-            copies.append(pltpu.make_async_copy(result.at[o, k], out_ref.at[o, k], sems.at[o, k]))
-            copies[-1].start()
+    blocks = [(k, o) for k in range(SLOTS) for o in range(OPS)]
+    mix(*blocks[0], 0)
+    for i, (k, o) in enumerate(blocks):
+        if i + 1 < len(blocks):
+            mix(*blocks[i + 1], (i + 1) % OPS)
+        result[o, k] = jnp.dot(tra[k], mixed[i % OPS], preferred_element_type=jnp.float32).astype(jnp.bfloat16)
+        copies.append(pltpu.make_async_copy(result.at[o, k], out_ref.at[o, k], sems.at[o, k]))
+        copies[-1].start()
     for copy in copies:
         copy.wait()
 

time: 56.5 us -> 56.1 us (level)
  no operation moved by 1% of the time
where the time goes in v3:
time: 56.1 us; the launch traced here: 55.9 us
  Pallas kernels  55.8 us (99%)
    pallas_call x1, Pallas kernels, local(): pl.pallas_call(gather, name='gather', out_shape=[pltpu.VMEM((NX * NZ, SLO...  50.8 us
    pallas_call x1, Pallas kernels, local(): pl.pallas_call(products, name='products', out_shape=jax.ShapeDtypeStruct(...  5.04 us

profile of v3, /device:TPU:8, one launch (start us, length us, event | category | flops | bytes accessed | tf_op | source)
XLA Modules:
  0.0 55.9 jit_solution(7310650964620579457)
XLA Ops:
  0.0 0.0 copy-start
  0.0 0.0 copy-start.2
  0.0 0.0 copy-start.1
  0.0 50.8 %gather.1 = (bf16[128,4,16,128]{3,2,1,0:T(8,128)(2,1)S(1)}, bf16[3,2,256,256]{3,2,1,0:T(8,128)(2,1)S(1)}) custom-call(bf16[3,4,256,256]{3,2,1,0:T(8,128)(2,1)} %own.1, bf16[4,8,256]{2,1,0:T(8,128)(2,1)} %site_in.1, s32[32]{0:T(128)} %sizes_in.1), custom_call_target="tpu_custom_call" | custom-call | bytes 6000000 | tf_op jit(solution)/shard_map/gather/pallas_call | solution.py:321
  50.8 0.0 copy-done
  50.8 0.0 copy-done.2
  50.8 0.0 copy-done.1
  50.8 5.0 %products.1 = bf16[3,4,256,256]{3,2,1,0:T(8,128)(2,1)} custom-call(bf16[3,4,256,256]{3,2,1,0:T(8,128)(2,1)S(1)} %copy-done, bf16[128,4,16,128]{3,2,1,0:T(8,128)(2,1)S(1)} %get-tuple-element.7.buf, bf16[3,2,256,256]{3,2,1,0:T(8,128)(2,1)S(1)} %get-tuple-element.8.halo, f32[3,6]{1,0:T(4,128)S(1)} %copy-done.1, s32[3,6]{1,0:T(4,128)S(1)} %copy-done.2), custom_call_target="tpu_custom_call" | custom-call | flops 3221225472 | bytes 3145728 | tf_op jit(solution)/shard_map/products/pallas_call | solution.py:348
Async XLA Ops:
  0.0 50.8 %copy-start = (bf16[3,4,256,256]{3,2,1,0:T(8,128)(2,1)S(1)}, bf16[3,4,256,256]{3,2,1,0:T(8,128)(2,1)}, u32[]{:S(2)}) copy-start(bf16[3,4,256,256]{3,2,1,0:T(8,128)(2,1)} %own.1) | copy-start | bytes 4718596
  0.0 50.8 %copy-start.2 = (s32[3,6]{1,0:T(4,128)S(1)}, s32[3,6]{1,0:T(4,128)}, u32[]{:S(2)}) copy-start(s32[3,6]{1,0:T(4,128)} %mask_ref.1) | copy-start | bytes 220
  0.0 50.8 %copy-start.1 = (f32[3,6]{1,0:T(4,128)S(1)}, f32[3,6]{1,0:T(4,128)}, u32[]{:S(2)}) copy-start(f32[3,6]{1,0:T(4,128)} %values_ref.1) | copy-start | bytes 220

commit v4 on v3

--- a/solution.py
+++ b/solution.py
@@ -11,134 +11,134 @@
 ROOT = 15
 
 PLAN = (
-    (0, 15, (11, 19, 47, 110, 49, 14, 16, 45, 79, 111)),
-    (0, 47, (48,)),
-    (0, 14, (12, 46)),
-    (0, 16, (18, 17, 112)),
-    (0, 111, ()),
-    (0, 110, (77, 109)),
+    (0, 15, (11, 16, 19, 13, 113, 47, 111, 79)),
+    (0, 16, (20, 80, 48, 112)),
+    (0, 47, (46, 78)),
+    (0, 111, (110,)),
+    (0, 13, (12, 77, 45, 109)),
     (0, 79, ()),
-    (0, 49, (50, 81)),
-    (0, 11, (7, 75, 10, 43, 107)),
-    (0, 19, (27, 119, 20, 115)),
+    (0, 113, (114, 49, 17, 81)),
+    (0, 11, (8, 107, 43)),
+    (0, 19, (27, 115, 50, 51)),
+    (0, 48, ()),
+    (0, 112, ()),
+    (0, 46, (14,)),
+    (0, 110, ()),
+    (0, 80, ()),
+    (0, 12, (9, 76, 44, 108)),
+    (0, 109, ()),
     (0, 45, ()),
-    (0, 48, (78,)),
-    (0, 46, ()),
-    (0, 112, ()),
+    (0, 78, ()),
+    (0, 114, (18, 82)),
+    (0, 81, ()),
     (0, 17, ()),
-    (0, 12, (44, 108)),
-    (0, 18, (114,)),
-    (0, 109, ()),
-    (0, 77, (13, 76)),
-    (0, 50, (82,)),
-    (0, 81, (113,)),
-    (0, 43, ()),
-    (0, 10, (8, 9, 74, 42, 106)),
-    (0, 20, (52, 53, 116)),
-    (0, 107, ()),
-    (0, 115, (117, 51, 83)),
-    (0, 75, (73,)),
+    (0, 20, (21, 84, 52, 116)),
+    (0, 77, ()),
+    (0, 107, (106,)),
+    (0, 43, (75,)),
+    (0, 49, ()),
+    (0, 115, (83,)),
+    (0, 8, (2, 72, 5, 40, 104)),
+    (0, 14, ()),
+    (0, 51, ()),
+    (0, 50, ()),
+    (0, 108, ()),
     (0, 44, ()),
-    (0, 108, ()),
-    (0, 7, (3, 39, 4, 103)),
-    (0, 114, ()),
-    (0, 78, (80,)),
+    (0, 18, ()),
+    (0, 76, ()),
     (0, 82, ()),
-    (0, 76, ()),
-    (0, 113, ()),
-    (0, 13, ()),
-    (0, 119, (120, 24, 22, 87, 55, 121, 23)),
-    (0, 9, (105,)),
-    (0, 106, ()),
-    (0, 52, (84,)),
+    (0, 21, (23, 22, 53, 117)),
+    (0, 9, (73, 10, 41, 105)),
     (0, 116, ()),
+    (0, 52, ()),
+    (0, 106, (42, 74)),
+    (0, 83, ()),
+    (0, 75, ()),
+    (0, 84, (85,)),
+    (0, 104, ()),
+    (0, 40, ()),
+    (0, 72, (71, 7)),
+    (0, 27, (29, 58, 123, 26, 28, 59)),
+    (0, 53, (54,)),
+    (0, 117, ()),
+    (0, 5, (69, 4, 6, 37, 101)),
+    (0, 22, (118,)),
+    (0, 41, ()),
+    (0, 105, ()),
+    (0, 10, ()),
+    (0, 23, (24, 55, 119)),
+    (0, 74, ()),
+    (0, 73, ()),
+    (0, 85, (86,)),
     (0, 42, ()),
-    (0, 8, (104,)),
-    (0, 83, ()),
-    (0, 73, (41, 72)),
-    (0, 117, (21,)),
-    (0, 74, ()),
-    (0, 27, (30, 123, 28, 26, 61, 91, 59)),
-    (0, 103, (101, 71)),
-    (0, 39, (38,)),
-    (0, 53, ()),
-    (0, 51, ()),
+    (0, 2, (34, 0, 66, 1, 3, 98)),
+    (0, 71, (103,)),
+    (0, 123, (91, 122, 124)),
+    (0, 28, ()),
+    (0, 59, ()),
+    (0, 26, (25,)),
+    (0, 29, (63, 126, 61, 30, 125)),
+    (0, 118, ()),
+    (0, 58, (57,)),
+    (0, 54, ()),
+    (0, 37, ()),
+    (0, 4, (36, 100)),
+    (0, 101, ()),
+    (0, 6, (38,)),
+    (0, 55, ()),
+    (0, 7, (39,)),
+    (0, 119, ()),
+    (0, 24, (120, 56)),
+    (0, 69, (68, 70)),
+    (0, 34, (33,)),
+    (0, 86, (87,)),
+    (0, 98, ()),
+    (0, 1, (97,)),
+    (0, 3, (35, 99)),
+    (0, 103, (102,)),
+    (0, 91, (92,)),
+    (0, 122, (90, 121)),
+    (0, 124, ()),
+    (0, 66, (65, 67)),
+    (0, 0, (64, 31, 96)),
+    (0, 30, ()),
+    (0, 61, (60, 62, 93)),
+    (0, 25, ()),
+    (0, 125, ()),
+    (0, 36, ()),
+    (0, 57, (89,)),
+    (0, 100, ()),
+    (0, 126, (94, 127)),
+    (0, 38, ()),
+    (0, 68, ()),
     (0, 120, (88,)),
-    (0, 87, (86,)),
-    (0, 4, (36, 5, 100)),
-    (0, 105, ()),
-    (0, 80, ()),
-    (0, 23, ()),
-    (0, 3, (2, 97, 0, 99, 35)),
-    (0, 104, ()),
-    (0, 24, (56, 25)),
-    (0, 84, (85,)),
-    (0, 22, (54, 118)),
+    (0, 63, (95,)),
+    (0, 39, ()),
+    (0, 33, (32,)),
+    (0, 70, ()),
+    (0, 97, ()),
+    (0, 56, ()),
+    (0, 102, ()),
+    (0, 87, ()),
+    (0, 99, ()),
+    (0, 35, ()),
     (0, 121, ()),
-    (0, 55, ()),
-    (0, 41, (40,)),
-    (0, 72, ()),
-    (0, 21, ()),
-    (0, 123, (124, 125)),
-    (0, 28, (60,)),
-    (0, 71, ()),
-    (0, 38, (70, 6)),
-    (0, 59, ()),
-    (0, 26, (58, 122)),
-    (0, 88, (89,)),
-    (0, 101, (69,)),
-    (0, 30, (126, 95, 63, 29, 31, 62)),
-    (0, 91, ()),
-    (0, 36, (37, 68)),
-    (0, 86, ()),
-    (0, 100, ()),
-    (0, 5, ()),
-    (0, 2, (1,)),
-    (0, 56, (57,)),
-    (0, 61, ()),
-    (0, 35, (34, 67)),
-    (0, 99, (66, 98)),
-    (0, 25, ()),
-    (0, 40, ()),
-    (0, 54, ()),
-    (0, 118, ()),
-    (0, 85, ()),
-    (0, 60, (92,)),
-    (0, 124, (93,)),
-    (0, 6, ()),
-    (0, 70, (102,)),
-    (0, 97, (64, 65, 96)),
-    (0, 122, ()),
-    (0, 58, ()),
-    (0, 89, (90,)),
-    (0, 0, (32,)),
-    (0, 69, ()),
-    (0, 125, ()),
-    (0, 29, ()),
-    (0, 126, (94, 127)),
+    (0, 92, ()),
+    (0, 90, ()),
     (0, 31, ()),
+    (0, 67, ()),
+    (0, 93, ()),
+    (0, 96, ()),
+    (0, 65, ()),
     (0, 62, ()),
-    (0, 1, (33,)),
-    (0, 37, ()),
-    (0, 68, ()),
-    (0, 34, ()),
-    (0, 57, ()),
-    (0, 98, ()),
-    (0, 63, ()),
-    (0, 67, ()),
-    (0, 95, ()),
-    (0, 92, ()),
-    (0, 66, ()),
-    (0, 102, ()),
-    (0, 96, ()),
-    (0, 90, ()),
-    (0, 32, ()),
-    (0, 65, ()),
-    (0, 93, ()),
+    (0, 89, ()),
+    (0, 60, ()),
+    (0, 127, ()),
     (0, 64, ()),
     (0, 94, ()),
-    (0, 127, ()),
-    (0, 33, ()),
+    (0, 95, ()),
+    (0, 32, ()),
+    (0, 88, ()),
 )
 
 

time: 56.1 us -> 54 us (0.963)
  the two profiles are of different devices: /device:TPU:8 before, /device:TPU:2 now
where the time goes in v4:
time: 54 us; the launch traced here: 53.8 us
  Pallas kernels  53.7 us (99%)
    pallas_call x1, Pallas kernels, local(): pl.pallas_call(gather, name='gather', out_shape=[pltpu.VMEM((NX * NZ, SLO...  48.7 us
    pallas_call x1, Pallas kernels, local(): pl.pallas_call(products, name='products', out_shape=jax.ShapeDtypeStruct(...  5.04 us

profile of v4, /device:TPU:2, one launch (start us, length us, event | category | flops | bytes accessed | tf_op | source)
XLA Modules:
  0.0 53.8 jit_solution(13753156442880628120)
XLA Ops:
  0.0 0.0 copy-start
  0.0 0.0 copy-start.2
  0.0 0.0 copy-start.1
  0.0 48.7 %gather.1 = (bf16[128,4,16,128]{3,2,1,0:T(8,128)(2,1)S(1)}, bf16[3,2,256,256]{3,2,1,0:T(8,128)(2,1)S(1)}) custom-call(bf16[3,4,256,256]{3,2,1,0:T(8,128)(2,1)} %own.1, bf16[4,8,256]{2,1,0:T(8,128)(2,1)} %site_in.1, s32[32]{0:T(128)} %sizes_in.1), custom_call_target="tpu_custom_call" | custom-call | bytes 6000000 | tf_op jit(solution)/shard_map/gather/pallas_call | solution.py:321
  48.7 0.0 copy-done
  48.7 0.0 copy-done.2
  48.7 0.0 copy-done.1
  48.7 5.0 %products.1 = bf16[3,4,256,256]{3,2,1,0:T(8,128)(2,1)} custom-call(bf16[3,4,256,256]{3,2,1,0:T(8,128)(2,1)S(1)} %copy-done, bf16[128,4,16,128]{3,2,1,0:T(8,128)(2,1)S(1)} %get-tuple-element.7.buf, bf16[3,2,256,256]{3,2,1,0:T(8,128)(2,1)S(1)} %get-tuple-element.8.halo, f32[3,6]{1,0:T(4,128)S(1)} %copy-done.1, s32[3,6]{1,0:T(4,128)S(1)} %copy-done.2), custom_call_target="tpu_custom_call" | custom-call | flops 3221225472 | bytes 3145728 | tf_op jit(solution)/shard_map/products/pallas_call | solution.py:348
Async XLA Ops:
  0.0 48.7 %copy-start = (bf16[3,4,256,256]{3,2,1,0:T(8,128)(2,1)S(1)}, bf16[3,4,256,256]{3,2,1,0:T(8,128)(2,1)}, u32[]{:S(2)}) copy-start(bf16[3,4,256,256]{3,2,1,0:T(8,128)(2,1)} %own.1) | copy-start | bytes 4718596
  0.0 48.7 %copy-start.2 = (s32[3,6]{1,0:T(4,128)S(1)}, s32[3,6]{1,0:T(4,128)}, u32[]{:S(2)}) copy-start(s32[3,6]{1,0:T(4,128)} %mask_ref.1) | copy-start | bytes 220
  0.0 48.7 %copy-start.1 = (f32[3,6]{1,0:T(4,128)S(1)}, f32[3,6]{1,0:T(4,128)}, u32[]{:S(2)}) copy-start(f32[3,6]{1,0:T(4,128)} %values_ref.1) | copy-start | bytes 220

commit v5 on v4

--- a/solution.py
+++ b/solution.py
@@ -13,64 +13,64 @@
 PLAN = (
     (0, 15, (11, 16, 19, 13, 113, 47, 111, 79)),
     (0, 16, (20, 80, 48, 112)),
-    (0, 47, (46, 78)),
-    (0, 111, (110,)),
-    (0, 13, (12, 77, 45, 109)),
+    (0, 47, (46,)),
+    (0, 111, (78, 110)),
+    (0, 13, (12, 45, 109)),
     (0, 79, ()),
     (0, 113, (114, 49, 17, 81)),
     (0, 11, (8, 107, 43)),
-    (0, 19, (27, 115, 50, 51)),
     (0, 48, ()),
     (0, 112, ()),
     (0, 46, (14,)),
+    (0, 19, (27, 115, 50, 51)),
     (0, 110, ()),
     (0, 80, ()),
-    (0, 12, (9, 76, 44, 108)),
+    (0, 12, (9, 108, 44)),
+    (0, 45, (77,)),
     (0, 109, ()),
-    (0, 45, ()),
     (0, 78, ()),
     (0, 114, (18, 82)),
+    (0, 17, ()),
     (0, 81, ()),
-    (0, 17, ()),
     (0, 20, (21, 84, 52, 116)),
-    (0, 77, ()),
+    (0, 43, (75,)),
     (0, 107, (106,)),
-    (0, 43, (75,)),
     (0, 49, ()),
     (0, 115, (83,)),
     (0, 8, (2, 72, 5, 40, 104)),
     (0, 14, ()),
     (0, 51, ()),
     (0, 50, ()),
-    (0, 108, ()),
+    (0, 108, (76,)),
     (0, 44, ()),
+    (0, 77, ()),
+    (0, 82, ()),
     (0, 18, ()),
-    (0, 76, ()),
-    (0, 82, ()),
+    (0, 116, ()),
     (0, 21, (23, 22, 53, 117)),
+    (0, 106, (42, 74)),
+    (0, 52, ()),
     (0, 9, (73, 10, 41, 105)),
-    (0, 116, ()),
-    (0, 52, ()),
-    (0, 106, (42, 74)),
+    (0, 75, ()),
     (0, 83, ()),
-    (0, 75, ()),
     (0, 84, (85,)),
     (0, 104, ()),
     (0, 40, ()),
+    (0, 76, ()),
     (0, 72, (71, 7)),
     (0, 27, (29, 58, 123, 26, 28, 59)),
     (0, 53, (54,)),
     (0, 117, ()),
     (0, 5, (69, 4, 6, 37, 101)),
     (0, 22, (118,)),
+    (0, 74, ()),
+    (0, 10, ()),
     (0, 41, ()),
+    (0, 23, (24, 55, 119)),
     (0, 105, ()),
-    (0, 10, ()),
-    (0, 23, (24, 55, 119)),
-    (0, 74, ()),
+    (0, 42, ()),
+    (0, 85, (86,)),
     (0, 73, ()),
-    (0, 85, (86,)),
-    (0, 42, ()),
     (0, 2, (34, 0, 66, 1, 3, 98)),
     (0, 71, (103,)),
     (0, 123, (91, 122, 124)),
@@ -80,11 +80,11 @@
     (0, 29, (63, 126, 61, 30, 125)),
     (0, 118, ()),
     (0, 58, (57,)),
-    (0, 54, ()),
+    (0, 6, (38,)),
     (0, 37, ()),
     (0, 4, (36, 100)),
     (0, 101, ()),
-    (0, 6, (38,)),
+    (0, 54, ()),
     (0, 55, ()),
     (0, 7, (39,)),
     (0, 119, ()),
@@ -107,12 +107,12 @@
     (0, 125, ()),
     (0, 36, ()),
     (0, 57, (89,)),
+    (0, 126, (94, 127)),
     (0, 100, ()),
-    (0, 126, (94, 127)),
     (0, 38, ()),
     (0, 68, ()),
+    (0, 63, (95,)),
     (0, 120, (88,)),
-    (0, 63, (95,)),
     (0, 39, ()),
     (0, 33, (32,)),
     (0, 70, ()),
@@ -133,8 +133,8 @@
     (0, 62, ()),
     (0, 89, ()),
     (0, 60, ()),
+    (0, 64, ()),
     (0, 127, ()),
-    (0, 64, ()),
     (0, 94, ()),
     (0, 95, ()),
     (0, 32, ()),

time: 54 us -> 54.8 us (1.015)
  Pallas kernels: 53.7 us -> 54.5 us
    pallas_call x1, Pallas kernels: 48.7 us -> 49.5 us  [local(): pl.pallas_call(gather, name='gather', out_shape=[pltpu.VMEM((NX * NZ, SLO...]
where the time goes in v5:
time: 54.8 us; the launch traced here: 54.6 us
  Pallas kernels  54.5 us (99%)
    pallas_call x1, Pallas kernels, local(): pl.pallas_call(gather, name='gather', out_shape=[pltpu.VMEM((NX * NZ, SLO...  49.5 us
    pallas_call x1, Pallas kernels, local(): pl.pallas_call(products, name='products', out_shape=jax.ShapeDtypeStruct(...  5.03 us

profile of v5, /device:TPU:2, one launch (start us, length us, event | category | flops | bytes accessed | tf_op | source)
XLA Modules:
  0.0 54.6 jit_solution(18405110034901428250)
XLA Ops:
  0.0 0.0 copy-start
  0.0 0.0 copy-start.2
  0.0 0.0 copy-start.1
  0.0 49.5 %gather.1 = (bf16[128,4,16,128]{3,2,1,0:T(8,128)(2,1)S(1)}, bf16[3,2,256,256]{3,2,1,0:T(8,128)(2,1)S(1)}) custom-call(bf16[3,4,256,256]{3,2,1,0:T(8,128)(2,1)} %own.1, bf16[4,8,256]{2,1,0:T(8,128)(2,1)} %site_in.1, s32[32]{0:T(128)} %sizes_in.1), custom_call_target="tpu_custom_call" | custom-call | bytes 6000000 | tf_op jit(solution)/shard_map/gather/pallas_call | solution.py:321
  49.5 0.0 copy-done
  49.5 0.0 copy-done.2
  49.5 0.0 copy-done.1
  49.5 5.0 %products.1 = bf16[3,4,256,256]{3,2,1,0:T(8,128)(2,1)} custom-call(bf16[3,4,256,256]{3,2,1,0:T(8,128)(2,1)S(1)} %copy-done, bf16[128,4,16,128]{3,2,1,0:T(8,128)(2,1)S(1)} %get-tuple-element.7.buf, bf16[3,2,256,256]{3,2,1,0:T(8,128)(2,1)S(1)} %get-tuple-element.8.halo, f32[3,6]{1,0:T(4,128)S(1)} %copy-done.1, s32[3,6]{1,0:T(4,128)S(1)} %copy-done.2), custom_call_target="tpu_custom_call" | custom-call | flops 3221225472 | bytes 3145728 | tf_op jit(solution)/shard_map/products/pallas_call | solution.py:348
Async XLA Ops:
  0.0 49.5 %copy-start = (bf16[3,4,256,256]{3,2,1,0:T(8,128)(2,1)S(1)}, bf16[3,4,256,256]{3,2,1,0:T(8,128)(2,1)}, u32[]{:S(2)}) copy-start(bf16[3,4,256,256]{3,2,1,0:T(8,128)(2,1)} %own.1) | copy-start | bytes 4718596
  0.0 49.5 %copy-start.2 = (s32[3,6]{1,0:T(4,128)S(1)}, s32[3,6]{1,0:T(4,128)}, u32[]{:S(2)}) copy-start(s32[3,6]{1,0:T(4,128)} %mask_ref.1) | copy-start | bytes 220
  0.0 49.5 %copy-start.1 = (f32[3,6]{1,0:T(4,128)S(1)}, f32[3,6]{1,0:T(4,128)}, u32[]{:S(2)}) copy-start(f32[3,6]{1,0:T(4,128)} %values_ref.1) | copy-start | bytes 220
